TPU v7x, 32 devices: a whole 2x2x4 slice. The times are simulated.
32 devices in a mesh: groups: 2 (over y), layer: 4 (over z), latent: 4 (over x, core).
Axes of the slice: x: 2, y: 2, z: 4, core: 2. Of those that a mesh axis runs over, the one named last changes fastest.
Arguments:
- acts: bfloat16 [2048, 14336], P('groups', 'layer'), parts along dimension 0, may hold values from -96 to 96, as said below
- enc_weight: bfloat16 [14336, 8192], P('layer', ('groups', 'latent')), parts along dimension 1, may hold values from -0.046875 to 0.046875
- dec_weight: bfloat16 [8192, 14336], P(('groups', 'latent'), 'layer'), parts along dimension 0, may hold values from -0.09375 to 0.09375
- enc_bias: float32 [8192], P(('groups', 'latent')), parts along dimension 0, may hold values from -4 to 4
- dec_bias: float32 [28672], P(('groups', 'layer')), parts along dimension 0, may hold values from -3 to 3
Outputs:
- grad_enc: bfloat16 [14336, 8192], P('layer', ('groups', 'latent')), parts along dimension 1
- grad_dec: bfloat16 [8192, 14336], P(('groups', 'latent'), 'layer'), parts along dimension 0
- grad_benc: float32 [8192], P(('groups', 'latent')), parts along dimension 0
- grad_bdec: float32 [28672], P(('groups', 'layer')), parts along dimension 0
- loss: float32 [2], P('groups'), parts along dimension 0
There are 2 independent parts, one for each index of `groups`. A program takes and returns all parts, laid end to end along the dimension named above; each array names one. Nothing has to cross between parts.
Inputs may be any that keep to these rules, and one draw needn't show every extreme that they name: `acts`: residual activations; their scale differs between tokens, features and layers.
All inputs are finite; a program needn't handle non-finite values.
Results may differ from a plain program's by a relative error of at most 0.0056.
Values may be sent and summed in bfloat16 or wider, within the bound.
A program may use at most 192 MiB of HBM per device.

v0:
```python
import jax
import jax.numpy as jnp
from jax import lax
from jax.sharding import PartitionSpec as P

D = 3584
LAYERS = 4


def on_device(acts, enc_weight, dec_weight, enc_bias, dec_bias):
    tok_rows, width = acts.shape
    layer_count = lax.axis_size("layer")
    latent_count = lax.axis_size("latent")
    first_col = lax.axis_index("layer") * width
    col_layer = (first_col + jnp.arange(width, dtype=jnp.int32)) // D
    onehot = (col_layer[:, None] == jnp.arange(LAYERS, dtype=jnp.int32)[None, :]).astype(
        jnp.float32
    )
    dec_wide = dec_weight.astype(jnp.float32)
    part_squares = jnp.dot(dec_wide * dec_wide, onehot, precision=lax.Precision.HIGHEST)
    layer_squares = lax.psum(part_squares, "layer")
    norms = jnp.sqrt(layer_squares + 1e-06)
    weight = jnp.sum(norms, axis=1)
    partial_pre = jnp.dot(acts, enc_weight, preferred_element_type=jnp.float32)
    pre = lax.psum(partial_pre, "layer") + enc_bias
    feats = jnp.maximum(pre, 0.0).astype(jnp.bfloat16)
    active = feats > 0
    partial_recon = jnp.dot(feats, dec_weight, preferred_element_type=jnp.float32)
    recon = lax.psum(partial_recon, "latent") + dec_bias
    error = recon - acts.astype(jnp.float32)
    feats_wide = feats.astype(jnp.float32)
    mse_local = jnp.sum(error * error)
    sparse_local = jnp.sum(feats_wide * weight[None, :])
    totals = lax.psum((mse_local, sparse_local), ("layer", "latent"))
    total = totals[0] / latent_count + 4.0 * totals[1] / layer_count
    loss = (total / (tok_rows * LAYERS * D)).reshape(1)
    grad_error = (2.0 / tok_rows * error).astype(jnp.bfloat16)
    grad_bdec = jnp.sum(grad_error.astype(jnp.float32), axis=0)
    feat_total = jnp.sum(feats_wide, axis=0)
    outer = lax.dot_general(
        feats, grad_error, (((0,), (0,)), ((), ())), preferred_element_type=jnp.float32
    )
    col_norms = jnp.dot(norms, onehot.T, precision=lax.Precision.HIGHEST)
    grad_dec = (outer + 4.0 / tok_rows * feat_total[:, None] * dec_wide / col_norms).astype(
        jnp.bfloat16
    )
    partial_grad = lax.dot_general(
        grad_error, dec_weight, (((1,), (1,)), ((), ())), preferred_element_type=jnp.float32
    )
    penalty = 4.0 / tok_rows * weight[None, :]
    grad_share = lax.psum_scatter(partial_grad, "layer", scatter_dimension=0, tiled=True) + penalty
    share_rows = grad_share.shape[0]
    active_share = lax.dynamic_slice_in_dim(
        active, lax.axis_index("layer") * share_rows, share_rows, 0
    )
    pre_share = jnp.where(active_share, grad_share, 0.0).astype(jnp.bfloat16)
    grad_pre = lax.all_gather(pre_share, "layer", axis=0, tiled=True)
    grad_benc = jnp.sum(grad_pre.astype(jnp.float32), axis=0)
    grad_enc = lax.dot_general(
        acts, grad_pre, (((0,), (0,)), ((), ())), preferred_element_type=jnp.float32
    ).astype(jnp.bfloat16)
    return (grad_enc, grad_dec, grad_benc, grad_bdec, loss)


def solution(mesh):
    placed = (
        P("groups", "layer"),
        P("layer", ("groups", "latent")),
        P(("groups", "latent"), "layer"),
        P(("groups", "latent")),
        P(("groups", "layer")),
    )
    return jax.shard_map(
        on_device,
        mesh=mesh,
        in_specs=placed,
        out_specs=(
            P("layer", ("groups", "latent")),
            P(("groups", "latent"), "layer"),
            P(("groups", "latent")),
            P(("groups", "layer")),
            P("groups"),
        ),
        check_vma=False,
    )
```

profile of v0, /device:TPU:0, one launch (start us, length us, event | category | flops | bytes accessed | tf_op | source)
XLA Modules:
  0.0 648.5 jit_solution(5782707283187903380)
XLA Ops:
  7.2 0.0 all-reduce.4.cloned.1.call-start
  7.2 13.4 %fusion.13 = f32[1024,1024]{1,0:T(8,128)} fusion(bf16[1024,3584]{1,0:T(8,128)(2,1)} %param.5, bf16[3584,1024]{1,0:T(8,128)(2,1)} %param.6), kind=kOutput, calls=%fused_computation.33 | convolution fusion | flops 7516192768 | bytes 18874368 | tf_op jit(solution)/shard_map/dot_general | solution.py:24
  20.6 0.0 copy-start.3
  20.6 0.0 all-reduce.4.cloned.1.call-update
  20.7 0.0 all-reduce.6.cloned.1.call-start
  20.8 9.6 %fusion = f32[1024,4]{0,1:T(4,128)S(1)} fusion(bf16[1024,3584]{1,0:T(8,128)(2,1)} %param.7, s32[3584]{0:T(1024)S(1)} %add_select_fusion), kind=kOutput, calls=%fused_computation.2 | convolution fusion | flops 183515136 | bytes 7370752 | tf_op jit(solution)/shard_map/dot_general | solution.py:20
  30.4 22.1 %psum.37 = f32[1024,4]{0,1:T(4,128)S(1)} all-reduce(f32[1024,4]{0,1:T(4,128)S(1)} %fusion), channel_id=1, replica_groups=mesh['groups'=2,'layer'=4,'latent'=4] {'layer'}, use_global_device_ids=true, to_apply=%region_3.4 | all-reduce | flops 4096 | bytes 32768 | tf_op jit(solution)/shard_map/psum | solution.py:21
  52.5 126.4 %all-reduce.4.cloned.1.call-done = f32[1024,1024]{1,0:T(8,128)} async-done(((f32[1024,1024]{1,0:T(8,128)}), f32[1024,1024]{1,0:T(8,128)}) %all-reduce.4.cloned.1.call-update) | async-done | bytes 4194320 | tf_op jit(solution)/shard_map/psum | solution.py:25
  178.9 0.0 copy-done.3
  179.0 3.9 fusion.5
  182.9 13.4 %fusion.14 = f32[1024,3584]{1,0:T(8,128)} fusion(bf16[1024,1024]{1,0:T(8,128)(2,1)S(1)} %get-tuple-element.21, bf16[1024,3584]{1,0:T(8,128)(2,1)} %param.7), kind=kOutput, calls=%fused_computation.34 | convolution fusion | flops 7516192768 | bytes 24117248 | tf_op jit(solution)/shard_map/dot_general | solution.py:28
  196.3 0.0 copy-start.2
  196.3 0.0 all-reduce.6.cloned.1.call-update
  196.3 0.2 reduce-scatter.2.cloned.1.call-start
  196.5 253.5 %all-reduce.6.cloned.1.call-done = f32[1024,3584]{1,0:T(8,128)} async-done(((f32[1024,3584]{1,0:T(8,128)}), f32[1024,3584]{1,0:T(8,128)}) %all-reduce.6.cloned.1.call-update) | async-done | bytes 14680080 | tf_op jit(solution)/shard_map/psum | solution.py:29
  450.0 0.0 copy-done.2
  450.0 9.8 %convert_reduce_fusion = (f32[3584]{0:T(1024)}, bf16[1024,3584]{1,0:T(8,128)(2,1)S(1)}, f32[]{:T(128)}) fusion(bf16[1024,3584]{1,0:T(8,128)(2,1)} %param.5, f32[1024,3584]{1,0:T(8,128)} %all-reduce.6.cloned.1.call-done, f32[3584]{0:T(1024)S(1)} %copy-done.2), kind=kLoop, calls=%fused_computation.7 | loop fusion | flops 33026560 | bytes 29388804 | tf_op jit(solution)/shard_map/reduce_sum | solution.py:38
  459.9 0.0 copy-start
  459.9 3.0 copy-done
  462.9 11.3 %fusion.15 = f32[1024,1024]{1,0:T(8,128)} fusion(bf16[1024,3584]{1,0:T(8,128)(2,1)S(1)} %get-tuple-element.20, bf16[1024,3584]{1,0:T(8,128)(2,1)} %param.7), kind=kOutput, calls=%fused_computation.35 | convolution fusion | flops 7516192768 | bytes 18874368 | tf_op jit(solution)/shard_map/dot_general | solution.py:47
  474.2 0.0 reduce-scatter.2.cloned.1.call-update
  474.2 0.0 all-gather.2.cloned.1.call-start
  474.3 77.1 %reduce-scatter.2.cloned.1.call-done = f32[256,1024]{1,0:T(8,128)} async-done(((f32[1024,1024]{1,0:T(8,128)}), f32[256,1024]{1,0:T(8,128)}) %reduce-scatter.2.cloned.1.call-update) | async-done | bytes 1048592 | tf_op jit(solution)/shard_map/reduce_scatter | solution.py:51
  551.4 2.2 select_convert_fusion
  553.6 0.0 all-gather.2.cloned.1.call-update
  553.7 9.3 %fusion.6 = f32[1024,3584]{1,0:T(8,128)} fusion(s32[3584]{0:T(1024)S(1)} %add_select_fusion, f32[1024,4]{0,1:T(4,128)S(1)} %psum.37), kind=kOutput, calls=%fused_computation.19 | convolution fusion | flops 176179200 | bytes 14710784 | tf_op jit(solution)/shard_map/dot_general | solution.py:43
  562.9 34.8 %all-reduce = (f32[]{:T(128)}, f32[]{:T(128)}) all-reduce(f32[]{:T(128)} %get-tuple-element.22, f32[]{:T(128)} %get-tuple-element.15), channel_id=1, replica_groups=mesh['groups'=2,'layer'=4,'latent'=4] {'layer','latent'}, use_global_device_ids=true, to_apply=%region_9.10 | all-reduce | flops 2 | bytes 16 | tf_op jit(solution)/shard_map/psum | solution.py:34
  599.1 17.6 %fusion.3 = bf16[1024,3584]{1,0:T(8,128)(2,1)} fusion(f32[1024,3584]{1,0:T(8,128)} %fusion.6, bf16[1024,3584]{1,0:T(8,128)(2,1)} %param.7, bf16[1024,1024]{1,0:T(8,128)(2,1)S(1)} %get-tuple-element.21, bf16[1024,3584]{1,0:T(8,128)(2,1)} %copy-done, f32[1024]{0:T(1024)S(1)} %broadcast_multiply_fusion), kind=kOutput, calls=%fused_computation.5 | convolution fusion | flops 7534542848 | bytes 38801408 | tf_op jit(solution)/shard_map/dot_general | solution.py:40
  616.6 0.0 all-gather.2.cloned.1.call-done
  616.6 12.7 %fusion.4 = bf16[3584,1024]{0,1:T(8,128)(2,1)} fusion(bf16[1024,1024]{1,0:T(8,128)(2,1)} %all-gather.2.cloned.1.call-done, bf16[1024,3584]{1,0:T(8,128)(2,1)} %param.5), kind=kOutput, calls=%fused_computation.11 | convolution fusion | flops 7519862784 | bytes 16777216 | tf_op jit(solution)/shard_map/dot_general | solution.py:59
  629.3 0.0 copy-start.1
  629.3 10.5 %copy.11 = bf16[3584,1024]{1,0:T(8,128)(2,1)} copy(bf16[3584,1024]{0,1:T(8,128)(2,1)} %fusion.4) | data formatting | bytes 14680064
  639.9 0.0 copy-done.1
  639.9 1.0 convert_reduce_fusion.2
  (4 shorter events, 0.1 us)
Async XLA Ops:
  7.2 171.8 %all-reduce.4.cloned.1.call-start = ((), (), s32[]{:S(2)}) async-start(), calls=%async_computation.1 | async-start | bytes 8388608 | tf_op jit(solution)/shard_map/psum | solution.py:25
  20.6 158.3 %copy-start.3 = (f32[1024]{0:T(1024)S(1)}, f32[1024]{0:T(1024)}, u32[]{:S(2)}) copy-start(f32[1024]{0:T(1024)} %param.8) | copy-start | bytes 12292
  20.7 429.4 %all-reduce.6.cloned.1.call-start = ((), (), s32[]{:S(2)}) async-start(), calls=%async_computation.2 | async-start | bytes 29360128 | tf_op jit(solution)/shard_map/psum | solution.py:29
  196.3 253.8 %copy-start.2 = (f32[3584]{0:T(1024)S(1)}, f32[3584]{0:T(1024)}, u32[]{:S(2)}) copy-start(f32[3584]{0:T(1024)} %param.9) | copy-start | bytes 43012
  196.3 355.1 %reduce-scatter.2.cloned.1.call-start = ((), (), s32[]{:S(2)}) async-start(), calls=%async_computation.3 | async-start | bytes 5242880 | tf_op jit(solution)/shard_map/reduce_scatter | solution.py:51
  459.9 3.0 copy-start
  474.2 142.4 %all-gather.2.cloned.1.call-start = ((), (), s32[]{:S(2)}) async-start(), calls=%async_computation.4 | async-start | bytes 2621440 | tf_op jit(solution)/shard_map/all_gather | solution.py:57
  629.3 10.5 %copy-start.1 = (bf16[1024,1024]{1,0:T(8,128)(2,1)S(1)}, bf16[1024,1024]{1,0:T(8,128)(2,1)}, u32[]{:S(2)}) copy-start(bf16[1024,1024]{1,0:T(8,128)(2,1)} %all-gather.2.cloned.1.call-done) | copy-start | bytes 6291460
Sparse Core Ops, SparseCore 0:
  20.8 158.1 all-reduce.3
  196.4 253.5 all-reduce.5
  474.4 76.9 reduce-scatter.1
  553.8 46.6 all-gather.1
where the time goes:
time: 649 us; the launch traced here: 648 us
  waiting for transfers between devices  457 us (70%)
  matrix products  87.3 us (13%)
  blocking collectives  57 us (9%)
  other arithmetic  16.9 us (3%)
  between operations  16.2 us (2%)
  local copies, waits for them, and re-layouts  13.6 us (2%)
    psum x1, waiting for transfers between devices, on_device(): recon = lax.psum(partial_recon, 'latent') + dec_bias  253 us
    psum x1, waiting for transfers between devices, on_device(): pre = lax.psum(partial_pre, 'layer') + enc_bias  126 us
    reduce_scatter x1, waiting for transfers between devices, on_device(): lax.psum_scatter(partial_grad, 'layer', scatter_dimension=0, tiled=True)  77.1 us
    psum x1, blocking collectives, on_device(): totals = lax.psum((mse_local, sparse_local), ('layer', 'latent'))  34.8 us
    psum x1, blocking collectives, on_device(): layer_squares = lax.psum(part_squares, 'layer')  22.1 us
    dot_general x1, matrix products, on_device(): lax.dot_general(feats, grad_error, (((0,), (0,)), ((), ())), preferred_el...  17.6 us
    unnamed x9, local copies, waits for them, and re-layouts  13.6 us
    dot_general x1, matrix products, on_device(): partial_pre = jnp.dot(acts, enc_weight, preferred_element_type=jnp.float32)  13.4 us
  transfers between devices with their start and end apart: 4, of which 3 were waited for; matrix products, arithmetic and copies ran while one was open for 6% of the time, Pallas kernels for 0%

commit v1 on v0

--- a/solution.py
+++ b/solution.py
@@ -1,10 +1,430 @@
+import functools
+
 import jax
 import jax.numpy as jnp
 from jax import lax
+from jax.experimental import pallas as pl
+from jax.experimental.pallas import tpu as pltpu
 from jax.sharding import PartitionSpec as P
 
 D = 3584
 LAYERS = 4
+PIECE = 128
+MESH = pl.DeviceIdType.MESH
+F32 = jnp.float32
+BF16 = jnp.bfloat16
+
+
+def tokens_kernel(
+    layer_count, acts_h, enc_h, dec_h, ebias, dbias, norms_in,
+    feats_h, gerr_h, gpre_h, mse, wsum,
+    enc_v, dec_v, acts_a, acts_e, part, pre_in, feats, out_half, own_half, core_in, x_in,
+    gerr, gpart, g_in, gpre, norms_all,
+    load_sem, acts_sem, acte_sem, store_sem, norm_send, norm_recv,
+    ps, pr, fs, fr, cs, cr, xs, xr, es, er, gs, gr, bs, br,
+):
+    tok_rows, width = acts_h.shape
+    lat = enc_h.shape[1]
+    T = PIECE
+    H = T // 2
+    NP = tok_rows // T
+    last = layer_count - 1
+    grp, z, k = lax.axis_index("groups"), lax.axis_index("layer"), lax.axis_index("latent")
+    core = k % 2
+    mate = (grp, z, k + 1 - 2 * core)
+    across = (grp, z, (k + 2) % 4)
+
+    def level(i):
+        return (grp, i, k)
+
+    enc_load = pltpu.make_async_copy(enc_h, enc_v, load_sem.at[0])
+    dec_load = pltpu.make_async_copy(dec_h, dec_v, load_sem.at[1])
+
+    def acts_load(p):
+        return pltpu.make_async_copy(
+            acts_h.at[pl.ds(p * T, T)], acts_a.at[p % 2], acts_sem.at[p % 2]
+        )
+
+    def acte_load(p):
+        return pltpu.make_async_copy(
+            acts_h.at[pl.ds(p * T + core * H, H)], acts_e.at[p % 2], acte_sem.at[p % 2]
+        )
+
+    enc_load.start()
+    acts_load(0).start()
+    dec_load.start()
+    mse[...] = jnp.zeros_like(mse)
+
+    barrier = pltpu.get_barrier_semaphore()
+    for step in range(1, layer_count):
+        pl.semaphore_signal(
+            barrier, inc=1, device_id=level((z + step) % layer_count), device_id_type=MESH
+        )
+    pl.semaphore_signal(barrier, inc=1, device_id=mate, device_id_type=MESH)
+    pl.semaphore_signal(barrier, inc=1, device_id=across, device_id_type=MESH)
+    pl.semaphore_wait(barrier, layer_count + 1)
+
+    def remote(src, dst, send, recv, dev):
+        return pltpu.make_async_remote_copy(
+            src_ref=src, dst_ref=dst, send_sem=send, recv_sem=recv,
+            device_id=dev, device_id_type=MESH,
+        )
+
+    def norm_copy(step):
+        return remote(
+            norms_in, norms_all.at[step], norm_send.at[step], norm_recv.at[step],
+            level((z + step) % layer_count),
+        )
+
+    for step in range(1, layer_count):
+        norm_copy(step).start()
+
+    def half_rows(way, p):
+        return pl.ds(pl.multiple_of(p * T + way * H, H), H)
+
+    def pos_of(way):
+        return z if way == 0 else last - z
+
+    def onward(way, by):
+        nxt = z + by if way == 0 else z - by
+        return level(jnp.clip(nxt, 0, last))
+
+    def pre_copy(way, p):
+        return remote(part.at[half_rows(way, p)], pre_in.at[half_rows(way, p)],
+                      ps.at[way, p], pr.at[way, p], onward(way, 1))
+
+    def feat_copy(way, p):
+        return remote(feats.at[half_rows(way, p)], feats.at[half_rows(way, p)],
+                      fs.at[way, p], fr.at[way, p], onward(way, -1))
+
+    def grad_copy(way, p):
+        return remote(gpart.at[half_rows(way, p)], g_in.at[half_rows(way, p)],
+                      gs.at[way, p], gr.at[way, p], onward(way, 1))
+
+    def gpre_copy(way, p):
+        return remote(gpre.at[half_rows(way, p)], gpre.at[half_rows(way, p)],
+                      bs.at[way, p], br.at[way, p], onward(way, -1))
+
+    def half_of(p):
+        return pl.ds(pl.multiple_of(p * H, H), H)
+
+    def core_copy(p):
+        return remote(out_half.at[half_of(p)], core_in.at[half_of(p)], cs.at[p], cr.at[p], mate)
+
+    def x_copy(p):
+        return remote(own_half.at[half_of(p)], x_in.at[half_of(p)], xs.at[p], xr.at[p], across)
+
+    def err_copy(p):
+        rows = pl.ds(pl.multiple_of(p * T + core * H, H), H)
+        return remote(gerr.at[rows], gerr.at[rows], es.at[p], er.at[p], mate)
+
+    def piece_rows(p):
+        return pl.ds(pl.multiple_of(p * T, T), T)
+
+    def store(which, p):
+        src, dst = ((feats, feats_h), (gerr, gerr_h), (gpre, gpre_h))[which]
+        return pltpu.make_async_copy(
+            src.at[piece_rows(p)], dst.at[piece_rows(p)], store_sem.at[which, p]
+        )
+
+    def valid(p):
+        return jnp.logical_and(p >= 0, p < NP)
+
+    def pre_chain(t, first):
+        for way in range(2):
+            pos = pos_of(way)
+            p = t - pos
+            here = pos == 0 if first else pos > 0
+
+            @pl.when(jnp.logical_and(valid(p), here))
+            def _():
+                rows = half_rows(way, p)
+                if not first:
+                    pre_copy(way, p).wait_recv()
+
+                    @pl.loop(0, lat // 256)
+                    def _(n):
+                        cols = pl.ds(pl.multiple_of(n * 256, 256), 256)
+                        part[rows, cols] += pre_in[rows, cols]
+
+                    @pl.when(pos < last)
+                    def _():
+                        pre_copy(way, p).start()
+
+                    @pl.when(pos == last)
+                    def _():
+                        @pl.loop(0, lat // 256)
+                        def _(n):
+                            cols = pl.ds(pl.multiple_of(n * 256, 256), 256)
+                            feats[rows, cols] = jnp.maximum(
+                                part[rows, cols] + ebias[:, cols], 0.0
+                            ).astype(BF16)
+                        feat_copy(way, p).start()
+                else:
+                    pre_copy(way, p).start()
+
+    def grad_chain(t, first):
+        for way in range(2):
+            pos = pos_of(way)
+            p = t - pos
+            here = pos == 0 if first else pos > 0
+
+            @pl.when(jnp.logical_and(valid(p), here))
+            def _():
+                rows = half_rows(way, p)
+                if not first:
+                    grad_copy(way, p).wait_recv()
+
+                    @pl.when(pos < last)
+                    def _():
+                        @pl.loop(0, lat // 256)
+                        def _(n):
+                            cols = pl.ds(pl.multiple_of(n * 256, 256), 256)
+                            gpart[rows, cols] = (
+                                gpart[rows, cols].astype(F32) + g_in[rows, cols].astype(F32)
+                            ).astype(BF16)
+                        grad_copy(way, p).start()
+
+                    @pl.when(pos == last)
+                    def _():
+                        @pl.loop(0, lat // 256)
+                        def _(n):
+                            cols = pl.ds(pl.multiple_of(n * 256, 256), 256)
+                            total = (
+                                gpart[rows, cols].astype(F32)
+                                + g_in[rows, cols].astype(F32)
+                                + 4.0 / tok_rows * wsum[0:1, cols]
+                            )
+                            live = feats[rows, cols].astype(F32) > 0.0
+                            gpre[rows, cols] = jnp.where(live, total, 0.0).astype(BF16)
+                        gpre_copy(way, p).start()
+                else:
+                    grad_copy(way, p).start()
+
+    def back(t, copy):
+        for way in range(2):
+            pos = pos_of(way)
+            p = t - (2 * last - pos)
+
+            @pl.when(jnp.logical_and(valid(p), pos < last))
+            def _():
+                copy(way, p).wait_recv()
+
+                @pl.when(pos > 0)
+                def _():
+                    copy(way, p).start()
+
+    enc_load.wait()
+    LR = 2 * last + 1
+    LC, LX, LG = LR + 1, LR + 2, LR + 3
+
+    @pl.loop(0, NP + LG + 2 * last + 1)
+    def _(t):
+        @pl.when(t == LR)
+        def _():
+            dec_load.wait()
+            total = norms_in[...]
+            for step in range(1, layer_count):
+                norm_copy(step).wait_recv()
+                total = total + norms_all[step]
+            wsum[...] = total
+
+        back(t - LG, gpre_copy)
+        p_done = t - LG - 2 * last
+
+        @pl.when(valid(p_done))
+        def _():
+            store(2, p_done).start()
+
+        grad_chain(t - LG, False)
+        back(t, feat_copy)
+        pre_chain(t, False)
+
+        p_x = t - LX
+
+        @pl.when(valid(p_x))
+        def _():
+            x_copy(p_x).wait_recv()
+            acte_load(p_x).wait()
+            rows = half_of(p_x)
+            grows = pl.ds(pl.multiple_of(p_x * T + core * H, H), H)
+
+            @pl.loop(0, width // 256)
+            def _(n):
+                cols = pl.ds(pl.multiple_of(n * 256, 256), 256)
+                error = (
+                    own_half[rows, cols].astype(F32) + x_in[rows, cols].astype(F32)
+                    + dbias[:, cols] - acts_e[p_x % 2, :, cols].astype(F32)
+                )
+                mse[:, cols] += jnp.sum((error * error).reshape(H // 8, 8, 256), axis=0)
+                gerr[grows, cols] = (2.0 / tok_rows * error).astype(BF16)
+            err_copy(p_x).start()
+
+        p_c = t - LC
+
+        @pl.when(valid(p_c))
+        def _():
+            acte_load(p_c).start()
+            core_copy(p_c).wait_recv()
+            rows = half_of(p_c)
+
+            @pl.loop(0, width // 256)
+            def _(n):
+                cols = pl.ds(pl.multiple_of(n * 256, 256), 256)
+                own_half[rows, cols] = (
+                    own_half[rows, cols].astype(F32) + core_in[rows, cols].astype(F32)
+                ).astype(BF16)
+            x_copy(p_c).start()
+
+        @pl.when(t < NP)
+        def _():
+            acts_load(t).wait()
+
+            @pl.when(t + 1 < NP)
+            def _():
+                acts_load(t + 1).start()
+
+            rows = piece_rows(t)
+
+            @pl.loop(0, lat // 256)
+            def _(n):
+                cols = pl.ds(pl.multiple_of(n * 256, 256), 256)
+                part[rows, cols] = jnp.dot(
+                    acts_a[t % 2], enc_v[:, cols], preferred_element_type=F32
+                )
+        pre_chain(t, True)
+
+        p_r = t - LR
+
+        @pl.when(valid(p_r))
+        def _():
+            store(0, p_r).start()
+            mine = pl.ds(pl.multiple_of(p_r * T + core * H, H), H)
+            other = pl.ds(pl.multiple_of(p_r * T + (1 - core) * H, H), H)
+            rows = half_of(p_r)
+
+            @pl.loop(0, width // 512)
+            def _(n):
+                cols = pl.ds(pl.multiple_of(n * 512, 512), 512)
+                both = jnp.concatenate([feats[mine, :], feats[other, :]], axis=0)
+                made = jnp.dot(both, dec_v[:, cols], preferred_element_type=F32)
+                own_half[rows, cols] = made[:H].astype(BF16)
+                out_half[rows, cols] = made[H:].astype(BF16)
+            core_copy(p_r).start()
+
+        p_g = t - LG
+
+        @pl.when(valid(p_g))
+        def _():
+            err_copy(p_g).wait_recv()
+            store(1, p_g).start()
+            rows = piece_rows(p_g)
+
+            @pl.loop(0, lat // 256)
+            def _(n):
+                cols = pl.ds(pl.multiple_of(n * 256, 256), 256)
+                gpart[rows, cols] = lax.dot_general(
+                    gerr[rows, :], dec_v[cols, :], (((1,), (1,)), ((), ())),
+                    preferred_element_type=F32,
+                ).astype(BF16)
+        grad_chain(t - LG, True)
+
+    for step in range(1, layer_count):
+        norm_copy(step).wait_send()
+
+    @pl.loop(0, NP)
+    def _(p):
+        for which in range(3):
+            store(which, p).wait()
+        core_copy(p).wait_send()
+        x_copy(p).wait_send()
+        err_copy(p).wait_send()
+        for way in range(2):
+            pos = pos_of(way)
+
+            @pl.when(pos < last)
+            def _():
+                pre_copy(way, p).wait_send()
+                grad_copy(way, p).wait_send()
+
+            @pl.when(pos > 0)
+            def _():
+                feat_copy(way, p).wait_send()
+                gpre_copy(way, p).wait_send()
+
+
+def on_device_kernel(acts, enc_weight, dec_weight, enc_bias, dec_bias):
+    tok_rows, width = acts.shape
+    lat = enc_weight.shape[1]
+    layer_count = lax.axis_size("layer")
+    dec_wide = dec_weight.astype(F32)
+    norms = jnp.sqrt(jnp.sum(dec_wide * dec_wide, axis=1) + 1e-06)
+    half = tok_rows // 2
+    pieces = tok_rows // PIECE
+    dma = pltpu.SemaphoreType.DMA
+    vm = pl.BlockSpec(memory_space=pltpu.VMEM)
+    hb = pl.BlockSpec(memory_space=pl.ANY)
+    feats, grad_error, grad_pre, mse, wsum = pl.pallas_call(
+        functools.partial(tokens_kernel, layer_count),
+        out_shape=(
+            jax.ShapeDtypeStruct((tok_rows, lat), BF16),
+            jax.ShapeDtypeStruct((tok_rows, width), BF16),
+            jax.ShapeDtypeStruct((tok_rows, lat), BF16),
+            jax.ShapeDtypeStruct((8, width), F32),
+            jax.ShapeDtypeStruct((8, lat), F32),
+        ),
+        in_specs=[hb, hb, hb, vm, vm, vm],
+        out_specs=(hb, hb, hb, vm, vm),
+        scratch_shapes=[
+            pltpu.VMEM((width, lat), BF16),
+            pltpu.VMEM((lat, width), BF16),
+            pltpu.VMEM((2, PIECE, width), BF16),
+            pltpu.VMEM((2, PIECE // 2, width), BF16),
+            pltpu.VMEM((tok_rows, lat), F32),
+            pltpu.VMEM((tok_rows, lat), F32),
+            pltpu.VMEM((tok_rows, lat), BF16),
+            pltpu.VMEM((half, width), BF16),
+            pltpu.VMEM((half, width), BF16),
+            pltpu.VMEM((half, width), BF16),
+            pltpu.VMEM((half, width), BF16),
+            pltpu.VMEM((tok_rows, width), BF16),
+            pltpu.VMEM((tok_rows, lat), BF16),
+            pltpu.VMEM((tok_rows, lat), BF16),
+            pltpu.VMEM((tok_rows, lat), BF16),
+            pltpu.VMEM((layer_count, 8, lat), F32),
+            dma((2,)), dma((2,)), dma((2,)), dma((3, pieces)),
+            dma((layer_count,)), dma((layer_count,)),
+            dma((2, pieces)), dma((2, pieces)), dma((2, pieces)), dma((2, pieces)),
+            dma((pieces,)), dma((pieces,)), dma((pieces,)), dma((pieces,)),
+            dma((pieces,)), dma((pieces,)),
+            dma((2, pieces)), dma((2, pieces)), dma((2, pieces)), dma((2, pieces)),
+        ],
+        compiler_params=pltpu.CompilerParams(
+            collective_id=0, has_side_effects=True, vmem_limit_bytes=62 * 1024 * 1024
+        ),
+        cost_estimate=pl.CostEstimate(
+            flops=6 * tok_rows * width * lat, bytes_accessed=8 * tok_rows * width, transcendentals=0
+        ),
+    )(
+        acts, enc_weight, dec_weight, enc_bias.reshape(1, lat), dec_bias.reshape(1, width),
+        jnp.broadcast_to(norms[None, :], (8, lat)),
+    )
+    feat_total = jnp.sum(feats.astype(F32), axis=0)
+    sparse_local = jnp.sum(feat_total * wsum[0])
+    totals = lax.psum(jnp.stack([jnp.sum(mse), sparse_local]), ("layer", "latent"))
+    total = totals[0] / 2 + 4.0 * totals[1] / layer_count
+    loss = (total / (tok_rows * LAYERS * D)).reshape(1)
+    grad_bdec = jnp.sum(grad_error.astype(F32), axis=0)
+    outer = lax.dot_general(
+        feats, grad_error, (((0,), (0,)), ((), ())), preferred_element_type=F32
+    )
+    coef = 4.0 / tok_rows * feat_total / norms
+    grad_dec = (outer + coef[:, None] * dec_wide).astype(BF16)
+    grad_benc = jnp.sum(grad_pre.astype(F32), axis=0)
+    grad_enc = lax.dot_general(
+        acts, grad_pre, (((0,), (0,)), ((), ())), preferred_element_type=F32
+    ).astype(BF16)
+    return (grad_enc, grad_dec, grad_benc, grad_bdec, loss)
 
 
 def on_device(acts, enc_weight, dec_weight, enc_bias, dec_bias):
@@ -70,8 +490,9 @@
         P(("groups", "latent")),
         P(("groups", "layer")),
     )
+    plain = mesh.shape["layer"] != LAYERS or mesh.shape["latent"] != 4
     return jax.shard_map(
-        on_device,
+        on_device if plain else on_device_kernel,
         mesh=mesh,
         in_specs=placed,
         out_specs=(

time: 649 us -> 277 us (0.43)
  waiting for transfers between devices: 457 us -> 0 us
  Pallas kernels: 0 us -> 191 us
  matrix products: 87.3 us -> 22.7 us
  blocking collectives: 57 us -> 29.6 us
  between operations: 16.2 us -> 3.63 us
    psum x2 -> x0, waiting for transfers between devices: 380 us -> none  [the longest x1 253 us: on_device(): recon = lax.psum(partial_recon, 'latent') + dec_bias]
    pallas_call x0 -> x1, Pallas kernels: none -> 191 us  [on_device_kernel(): pl.pallas_call(functools.partial(tokens_kernel, layer_count), out_shape=(...]
    reduce_scatter x1 -> x0, waiting for transfers between devices: 77.1 us -> none  [on_device(): lax.psum_scatter(partial_grad, 'layer', scatter_dimension=0, tiled=True)]
    dot_general x7 -> x2, matrix products: 87.3 us -> 22.7 us  [the longest x1 12.5 us: on_device_kernel(): lax.dot_general(feats, grad_error, (((0,), (0,)), ((), ())), preferred_el...]
    psum x2 -> x1, blocking collectives: 57 us -> 29.6 us  [on_device_kernel(): lax.psum(jnp.stack([jnp.sum(mse), sparse_local]), ('layer', 'latent'))]
    unnamed x9 -> x13, local copies, waits for them, and re-layouts: 13.6 us -> 10.4 us
    reduce_sum x4 -> x5, other arithmetic: 14.7 us -> 15.4 us  [the longest x1 4.89 us: on_device_kernel(): grad_bdec = jnp.sum(grad_error.astype(F32), axis=0)]
  transfers between devices with their start and end apart: 4 -> 0, of which waited for: 3 -> 0; matrix products, arithmetic and copies ran while one was open for 6% -> 0% of each run, Pallas kernels for 0% -> 0%
where the time goes in v1:
time: 277 us; the launch traced here: 276 us
  Pallas kernels  191 us (69%)
  blocking collectives  29.6 us (11%)
  matrix products  22.7 us (8%)
  other arithmetic  16.8 us (6%)
  local copies, waits for them, and re-layouts  13 us (5%)
  between operations  3.63 us (1%)
    pallas_call x1, Pallas kernels, on_device_kernel(): pl.pallas_call(functools.partial(tokens_kernel, layer_count), out_shape=(...  191 us
    psum x1, blocking collectives, on_device_kernel(): lax.psum(jnp.stack([jnp.sum(mse), sparse_local]), ('layer', 'latent'))  29.6 us
    dot_general x1, matrix products, on_device_kernel(): lax.dot_general(feats, grad_error, (((0,), (0,)), ((), ())), preferred_el...  12.5 us
    unnamed x13, local copies, waits for them, and re-layouts  10.4 us
    dot_general x1, matrix products, on_device_kernel(): lax.dot_general(acts, grad_pre, (((0,), (0,)), ((), ())), preferred_eleme...  10.2 us

profile of v1, /device:TPU:0, one launch (start us, length us, event | category | flops | bytes accessed | tf_op | source)
XLA Modules:
  0.0 276.4 jit_solution(10630588213959465277)
XLA Ops:
  0.6 0.0 copy-start.3
  0.6 4.6 %fusion = f32[1024]{0:T(1024)S(1)} fusion(bf16[1024,3584]{1,0:T(8,128)(2,1)} %dec_h.1), kind=kLoop, calls=%fused_computation.2 | loop fusion | flops 11009024 | bytes 7344128 | tf_op jit(solution)/shard_map/reduce_sum | solution.py:361
  5.2 0.0 copy-done.3
  5.2 0.6 reshape.36.dbias
  5.9 0.6 broadcast_in_dim.2.norms_in
  6.5 190.7 %shard_map.92 = (bf16[1024,1024]{1,0:T(8,128)(2,1)}, bf16[1024,3584]{1,0:T(8,128)(2,1)}, bf16[1024,1024]{1,0:T(8,128)(2,1)}, f32[8,3584]{1,0:T(8,128)}, f32[8,1024]{1,0:T(8,128)}) custom-call(bf16[1024,3584]{1,0:T(8,128)(2,1)} %acts_h.1, bf16[3584,1024]{1,0:T(8,128)(2,1)} %enc_h.1, bf16[1024,3584]{1,0:T(8,128)(2,1)} %dec_h.1, f32[1,1024]{1,0:T(1,128)} %bitcast.13, ...), custom_call_target="tpu_custom_call" | custom-call | flops 22548578304 | bytes 29360128 | tf_op jit(solution)/shard_map/pallas_call | solution.py:367
  197.2 0.0 copy-start.2
  197.2 1.7 reduce_sum.58
  198.9 0.8 slice.9
  199.6 3.6 %convert_reduce_fusion.1 = (f32[1024]{0:T(1024)}, f32[1024]{0:T(1024)S(1)}) fusion(bf16[1024,1024]{1,0:T(8,128)(2,1)} %get-tuple-element.10, bf16[1024,1024]{1,0:T(8,128)(2,1)} %get-tuple-element.11), kind=kLoop, calls=%fused_computation.8 | loop fusion | flops 4192256 | bytes 4202496 | tf_op jit(solution)/shard_map/reduce_sum | solution.py:423
  203.3 0.6 multiply_reduce_fusion
  203.9 1.4 pad_maximum_fusion
  205.2 29.6 %psum.7 = f32[2]{0:T(128)S(1)} all-reduce(f32[2]{0:T(128)S(1)} %pad_maximum_fusion), channel_id=1, replica_groups=mesh['groups'=2,'layer'=4,'latent'=4] {'layer','latent'}, use_global_device_ids=true, to_apply=%region_6.0 | all-reduce | flops 2 | bytes 16 | tf_op jit(solution)/shard_map/psum | solution.py:414
  234.9 0.0 copy-start
  234.9 0.6 fusion.4
  237.3 0.0 slice-start
  237.3 4.9 %convert_reduce_fusion = f32[3584]{0:T(1024)} fusion(bf16[1024,3584]{1,0:T(8,128)(2,1)} %get-tuple-element.12), kind=kLoop, calls=%fused_computation.5 | loop fusion | flops 7336448 | bytes 7354368 | tf_op jit(solution)/shard_map/reduce_sum | solution.py:417
  242.2 0.0 copy-done.2
  242.2 0.0 copy-done
  242.2 0.0 copy-start.1
  242.2 0.0 slice-start.1
  242.2 12.5 %fusion.2 = bf16[1024,3584]{1,0:T(8,128)(2,1)} fusion(bf16[1024,3584]{1,0:T(8,128)(2,1)} %dec_h.1, bf16[1024,1024]{1,0:T(8,128)(2,1)S(1)} %copy-done.2, bf16[1024,3584]{1,0:T(8,128)(2,1)S(1)} %copy-done, f32[1024]{0:T(1024)S(1)} %get-tuple-element.21), kind=kOutput, calls=%fused_computation.4 | convolution fusion | flops 7530872832 | bytes 24121344 | tf_op jit(solution)/shard_map/dot_general | solution.py:418
  254.7 0.0 slice-done
  254.7 0.0 copy-done.1
  254.7 0.0 slice-done.1
  254.7 10.2 %fusion.3 = bf16[3584,1024]{0,1:T(8,128)(2,1)} fusion(bf16[1024,1024]{1,0:T(8,128)(2,1)S(1)} %copy-done.1, bf16[1024,3584]{1,0:T(8,128)(2,1)S(1)} %bitcast.12), kind=kOutput, calls=%fused_computation.7 | convolution fusion | flops 7519862784 | bytes 16777216 | tf_op jit(solution)/shard_map/dot_general | solution.py:424
  264.9 10.4 %copy.10 = bf16[3584,1024]{1,0:T(8,128)(2,1)} copy(bf16[3584,1024]{0,1:T(8,128)(2,1)} %fusion.3) | data formatting | bytes 14680064
  (2 shorter events, 0.0 us)
Async XLA Ops:
  0.6 4.6 %copy-start.3 = (f32[3584]{0:T(1024)S(1)}, f32[3584]{0:T(1024)}, u32[]{:S(2)}) copy-start(f32[3584]{0:T(1024)} %param.9) | copy-start | bytes 43012
  197.2 45.0 %copy-start.2 = (bf16[1024,1024]{1,0:T(8,128)(2,1)S(1)}, bf16[1024,1024]{1,0:T(8,128)(2,1)}, u32[]{:S(2)}) copy-start(bf16[1024,1024]{1,0:T(8,128)(2,1)} %get-tuple-element.11) | copy-start | bytes 6291460
  234.9 7.3 %copy-start = (bf16[1024,3584]{1,0:T(8,128)(2,1)S(1)}, bf16[1024,3584]{1,0:T(8,128)(2,1)}, u32[]{:S(2)}) copy-start(bf16[1024,3584]{1,0:T(8,128)(2,1)} %get-tuple-element.12) | copy-start | bytes 22020100
  237.3 17.4 %slice-start = ((s8[7340032]{0:T(1024)(128)(4,1)}), s8[4194304]{0:T(1024)(128)(4,1)S(1)}, s32[]{:S(2)}) async-start(s8[7340032]{0:T(1024)(128)(4,1)} %bitcast.11), calls=%async_computation | async-start | bytes 8388608
  242.2 12.5 %copy-start.1 = (bf16[1024,1024]{1,0:T(8,128)(2,1)S(1)}, bf16[1024,1024]{1,0:T(8,128)(2,1)}, u32[]{:S(2)}) copy-start(bf16[1024,1024]{1,0:T(8,128)(2,1)} %get-tuple-element.10) | copy-start | bytes 6291460
  242.2 12.5 %slice-start.1 = ((s8[7340032]{0:T(1024)(128)(4,1)}), s8[3145728]{0:T(1024)(128)(4,1)S(1)}, s32[]{:S(2)}) async-start(s8[7340032]{0:T(1024)(128)(4,1)} %bitcast.11), calls=%async_computation.1 | async-start | bytes 6291456

commit v2 on v1

--- a/solution.py
+++ b/solution.py
@@ -17,11 +17,12 @@
 
 def tokens_kernel(
     layer_count, acts_h, enc_h, dec_h, ebias, dbias, norms_in,
-    feats_h, gerr_h, gpre_h, mse, wsum,
+    feats_h, gerr_h, gpre_h, feat_sum, err_sum, gpre_sum, loss,
     enc_v, dec_v, acts_a, acts_e, part, pre_in, feats, out_half, own_half, core_in, x_in,
     gerr, gpart, g_in, gpre, norms_all,
+    mse, wsum, fsum, esum, bsum, lslots, lpair, lin,
     load_sem, acts_sem, acte_sem, store_sem, norm_send, norm_recv,
-    ps, pr, fs, fr, cs, cr, xs, xr, es, er, gs, gr, bs, br,
+    ps, pr, fs, fr, cs, cr, xs, xr, es, er, gs, gr, bs, br, ls, lr,
 ):
     tok_rows, width = acts_h.shape
     lat = enc_h.shape[1]
@@ -53,7 +54,8 @@
     enc_load.start()
     acts_load(0).start()
     dec_load.start()
-    mse[...] = jnp.zeros_like(mse)
+    for held in (mse, fsum, esum, bsum):
+        held[...] = jnp.zeros_like(held)
 
     barrier = pltpu.get_barrier_semaphore()
     for step in range(1, layer_count):
@@ -214,9 +216,17 @@
                 def _():
                     copy(way, p).start()
 
+    def loss_copy(step):
+        return remote(lslots.at[z], lslots.at[z], ls.at[step], lr.at[step],
+                      level((z + step) % layer_count))
+
+    def loss_pair(i):
+        return remote(lpair.at[i], lin.at[i], ls.at[layer_count + i], lr.at[layer_count + i],
+                      (mate, across)[i])
+
     enc_load.wait()
-    LR = 2 * last + 1
-    LC, LX, LG = LR + 1, LR + 2, LR + 3
+    LR = 2 * last
+    LC, LX, LG = LR + 1, LR + 2, LR + 2
 
     @pl.loop(0, NP + LG + 2 * last + 1)
     def _(t):
@@ -229,12 +239,50 @@
                 total = total + norms_all[step]
             wsum[...] = total
 
+        @pl.when(t == NP + LX)
+        def _():
+            mine = 0.5 * jnp.sum(mse[...]) + 4.0 / layer_count * jnp.sum(
+                jnp.sum(fsum[...], axis=0, keepdims=True) * wsum[0:1, :]
+            )
+            lslots[z] = jnp.full((8, 128), mine, F32)
+            for step in range(1, layer_count):
+                loss_copy(step).start()
+
+        @pl.when(t == NP + LX + 1)
+        def _():
+            for step in range(1, layer_count):
+                loss_copy(step).wait_recv()
+            total = lslots[0]
+            for i in range(1, layer_count):
+                total = total + lslots[i]
+            lpair[0] = total
+            loss_pair(0).start()
+
+        @pl.when(t == NP + LX + 2)
+        def _():
+            loss_pair(0).wait_recv()
+            lpair[1] = lpair[0] + lin[0]
+            loss_pair(1).start()
+
+        @pl.when(t == NP + LX + 3)
+        def _():
+            loss_pair(1).wait_recv()
+            loss[...] = (lpair[1] + lin[1]) / (tok_rows * LAYERS * D)
+
         back(t - LG, gpre_copy)
         p_done = t - LG - 2 * last
 
         @pl.when(valid(p_done))
         def _():
             store(2, p_done).start()
+            rows = piece_rows(p_done)
+
+            @pl.loop(0, lat // 256)
+            def _(n):
+                cols = pl.ds(pl.multiple_of(n * 256, 256), 256)
+                bsum[:, cols] += jnp.sum(
+                    gpre[rows, cols].astype(F32).reshape(T // 8, 8, 256), axis=0
+                )
 
         grad_chain(t - LG, False)
         back(t, feat_copy)
@@ -302,6 +350,14 @@
             mine = pl.ds(pl.multiple_of(p_r * T + core * H, H), H)
             other = pl.ds(pl.multiple_of(p_r * T + (1 - core) * H, H), H)
             rows = half_of(p_r)
+            whole = piece_rows(p_r)
+
+            @pl.loop(0, lat // 256)
+            def _(n):
+                cols = pl.ds(pl.multiple_of(n * 256, 256), 256)
+                fsum[:, cols] += jnp.sum(
+                    feats[whole, cols].astype(F32).reshape(T // 8, 8, 256), axis=0
+                )
 
             @pl.loop(0, width // 512)
             def _(n):
@@ -328,6 +384,25 @@
                     preferred_element_type=F32,
                 ).astype(BF16)
         grad_chain(t - LG, True)
+
+        @pl.when(valid(p_g))
+        def _():
+            rows = piece_rows(p_g)
+
+            @pl.loop(0, width // 256)
+            def _(n):
+                cols = pl.ds(pl.multiple_of(n * 256, 256), 256)
+                esum[:, cols] += jnp.sum(
+                    gerr[rows, cols].astype(F32).reshape(T // 8, 8, 256), axis=0
+                )
+
+    feat_sum[...] = jnp.sum(fsum[...], axis=0, keepdims=True)
+    err_sum[...] = jnp.sum(esum[...], axis=0, keepdims=True)
+    gpre_sum[...] = jnp.sum(bsum[...], axis=0, keepdims=True)
+    for i in range(2):
+        loss_pair(i).wait_send()
+    for step in range(1, layer_count):
+        loss_copy(step).wait_send()
 
     for step in range(1, layer_count):
         norm_copy(step).wait_send()
@@ -351,6 +426,12 @@
             def _():
                 feat_copy(way, p).wait_send()
                 gpre_copy(way, p).wait_send()
+
+
+def encoder_kernel(acts, gpre, out):
+    out[...] = lax.dot_general(
+        acts[...], gpre[...], (((0,), (0,)), ((), ())), preferred_element_type=F32
+    ).astype(BF16)
 
 
 def on_device_kernel(acts, enc_weight, dec_weight, enc_bias, dec_bias):
@@ -364,17 +445,19 @@
     dma = pltpu.SemaphoreType.DMA
     vm = pl.BlockSpec(memory_space=pltpu.VMEM)
     hb = pl.BlockSpec(memory_space=pl.ANY)
-    feats, grad_error, grad_pre, mse, wsum = pl.pallas_call(
+    feats, grad_error, grad_pre, feat_total, err_total, gpre_total, loss = pl.pallas_call(
         functools.partial(tokens_kernel, layer_count),
         out_shape=(
             jax.ShapeDtypeStruct((tok_rows, lat), BF16),
             jax.ShapeDtypeStruct((tok_rows, width), BF16),
             jax.ShapeDtypeStruct((tok_rows, lat), BF16),
-            jax.ShapeDtypeStruct((8, width), F32),
-            jax.ShapeDtypeStruct((8, lat), F32),
+            jax.ShapeDtypeStruct((1, lat), F32),
+            jax.ShapeDtypeStruct((1, width), F32),
+            jax.ShapeDtypeStruct((1, lat), F32),
+            jax.ShapeDtypeStruct((8, 128), F32),
         ),
         in_specs=[hb, hb, hb, vm, vm, vm],
-        out_specs=(hb, hb, hb, vm, vm),
+        out_specs=(hb, hb, hb, vm, vm, vm, vm),
         scratch_shapes=[
             pltpu.VMEM((width, lat), BF16),
             pltpu.VMEM((lat, width), BF16),
@@ -392,12 +475,21 @@
             pltpu.VMEM((tok_rows, lat), BF16),
             pltpu.VMEM((tok_rows, lat), BF16),
             pltpu.VMEM((layer_count, 8, lat), F32),
+            pltpu.VMEM((8, width), F32),
+            pltpu.VMEM((8, lat), F32),
+            pltpu.VMEM((8, lat), F32),
+            pltpu.VMEM((8, width), F32),
+            pltpu.VMEM((8, lat), F32),
+            pltpu.VMEM((layer_count, 8, 128), F32),
+            pltpu.VMEM((2, 8, 128), F32),
+            pltpu.VMEM((2, 8, 128), F32),
             dma((2,)), dma((2,)), dma((2,)), dma((3, pieces)),
             dma((layer_count,)), dma((layer_count,)),
             dma((2, pieces)), dma((2, pieces)), dma((2, pieces)), dma((2, pieces)),
             dma((pieces,)), dma((pieces,)), dma((pieces,)), dma((pieces,)),
             dma((pieces,)), dma((pieces,)),
             dma((2, pieces)), dma((2, pieces)), dma((2, pieces)), dma((2, pieces)),
+            dma((layer_count + 2,)), dma((layer_count + 2,)),
         ],
         compiler_params=pltpu.CompilerParams(
             collective_id=0, has_side_effects=True, vmem_limit_bytes=62 * 1024 * 1024
@@ -409,22 +501,27 @@
         acts, enc_weight, dec_weight, enc_bias.reshape(1, lat), dec_bias.reshape(1, width),
         jnp.broadcast_to(norms[None, :], (8, lat)),
     )
-    feat_total = jnp.sum(feats.astype(F32), axis=0)
-    sparse_local = jnp.sum(feat_total * wsum[0])
-    totals = lax.psum(jnp.stack([jnp.sum(mse), sparse_local]), ("layer", "latent"))
-    total = totals[0] / 2 + 4.0 * totals[1] / layer_count
-    loss = (total / (tok_rows * LAYERS * D)).reshape(1)
-    grad_bdec = jnp.sum(grad_error.astype(F32), axis=0)
     outer = lax.dot_general(
         feats, grad_error, (((0,), (0,)), ((), ())), preferred_element_type=F32
     )
-    coef = 4.0 / tok_rows * feat_total / norms
+    coef = 4.0 / tok_rows * feat_total[0] / norms
     grad_dec = (outer + coef[:, None] * dec_wide).astype(BF16)
-    grad_benc = jnp.sum(grad_pre.astype(F32), axis=0)
-    grad_enc = lax.dot_general(
-        acts, grad_pre, (((0,), (0,)), ((), ())), preferred_element_type=F32
-    ).astype(BF16)
-    return (grad_enc, grad_dec, grad_benc, grad_bdec, loss)
+    tile = 512
+    grad_enc = pl.pallas_call(
+        encoder_kernel,
+        grid=(width // tile,),
+        out_shape=jax.ShapeDtypeStruct((width, lat), BF16),
+        in_specs=[
+            pl.BlockSpec((tok_rows, tile), lambda i: (0, i)),
+            pl.BlockSpec((tok_rows, lat), lambda i: (0, 0)),
+        ],
+        out_specs=pl.BlockSpec((tile, lat), lambda i: (i, 0)),
+        compiler_params=pltpu.CompilerParams(vmem_limit_bytes=32 * 1024 * 1024),
+        cost_estimate=pl.CostEstimate(
+            flops=2 * tok_rows * width * lat, bytes_accessed=4 * tok_rows * width, transcendentals=0
+        ),
+    )(acts, grad_pre)
+    return (grad_enc, grad_dec, gpre_total[0], err_total[0], loss[0, 0:1])
 
 
 def on_device(acts, enc_weight, dec_weight, enc_bias, dec_bias):

time: 277 us -> 216 us (0.78)
  blocking collectives: 29.6 us -> 0 us
  other arithmetic: 16.8 us -> 5.92 us
  matrix products: 22.7 us -> 14.1 us
  local copies, waits for them, and re-layouts: 13 us -> 6.11 us
  between operations: 3.63 us -> 0.67 us
    psum x1 -> x0, blocking collectives: 29.6 us -> none  [on_device_kernel(): lax.psum(jnp.stack([jnp.sum(mse), sparse_local]), ('layer', 'latent'))]
    pallas_call x1, Pallas kernels: 191 us -> 178 us  [on_device_kernel(): pl.pallas_call(functools.partial(tokens_kernel, layer_count), out_shape=(...]
    reduce_sum x4 -> x0, other arithmetic: 10.8 us -> none  [the longest x1 4.89 us: on_device_kernel(): grad_bdec = jnp.sum(grad_error.astype(F32), axis=0)]
    pallas_call x0 -> x1, Pallas kernels: none -> 10.5 us  [on_device_kernel(): pl.pallas_call(encoder_kernel, grid=(width // tile,), out_shape=jax.Shape...]
    dot_general x1 -> x0, matrix products: 10.2 us -> none  [on_device_kernel(): lax.dot_general(acts, grad_pre, (((0,), (0,)), ((), ())), preferred_eleme...]
    unnamed x13 -> x11, local copies, waits for them, and re-layouts: 10.4 us -> 3.69 us
where the time goes in v2:
time: 216 us
  Pallas kernels  189 us (88%)
  matrix products  14.1 us (7%)
  local copies, waits for them, and re-layouts  6.11 us (3%)
  other arithmetic  5.92 us (3%)
    pallas_call x1, Pallas kernels, on_device_kernel(): pl.pallas_call(functools.partial(tokens_kernel, layer_count), out_shape=(...  178 us
    dot_general x1, matrix products, on_device_kernel(): lax.dot_general(feats, grad_error, (((0,), (0,)), ((), ())), preferred_el...  14.1 us
    pallas_call x1, Pallas kernels, on_device_kernel(): pl.pallas_call(encoder_kernel, grid=(width // tile,), out_shape=jax.Shape...  10.5 us
    reduce_sum x1, other arithmetic, on_device_kernel(): norms = jnp.sqrt(jnp.sum(dec_wide * dec_wide, axis=1) + 1e-06)  4.58 us

profile of v2, /device:TPU:0, one launch (start us, length us, event | category | flops | bytes accessed | tf_op | source)
XLA Modules:
  0.0 215.6 jit_solution(1656603034934068921)
XLA Ops:
  0.6 0.0 copy-start.2
  0.6 4.6 %fusion = f32[1024]{0:T(1024)S(1)} fusion(bf16[1024,3584]{1,0:T(8,128)(2,1)} %dec_h.1), kind=kLoop, calls=%fused_computation.2 | loop fusion | flops 11009024 | bytes 7344128 | tf_op jit(solution)/shard_map/reduce_sum | solution.py:442
  5.2 0.0 copy-done.2
  5.2 0.6 reshape.33.dbias
  5.9 0.6 broadcast_in_dim.2.norms_in
  6.5 178.3 %shard_map.92 = (bf16[1024,1024]{1,0:T(8,128)(2,1)}, bf16[1024,3584]{1,0:T(8,128)(2,1)}, bf16[1024,1024]{1,0:T(8,128)(2,1)}, f32[1,1024]{1,0:T(1,128)}, f32[1,35...) custom-call(bf16[1024,3584]{1,0:T(8,128)(2,1)} %acts.1, bf16[3584,1024]{1,0:T(8,128)(2,1)} %enc_h.1, ...), custom_call_target="tpu_custom_call" | custom-call | flops 22548578304 | bytes 29360128 | tf_op jit(solution)/shard_map/pallas_call | solution.py:448
  184.8 1.2 slice.3
  186.0 0.7 broadcast_multiply_fusion
  186.7 0.0 copy-start.3
  186.7 0.0 copy-start.1
  186.7 14.1 %fusion.2 = bf16[1024,3584]{1,0:T(8,128)(2,1)} fusion(bf16[1024,3584]{1,0:T(8,128)(2,1)} %dec_h.1, bf16[1024,1024]{1,0:T(8,128)(2,1)} %get-tuple-element.13, bf16[1024,3584]{1,0:T(8,128)(2,1)} %get-tuple-element.14, f32[1024]{0:T(1024)S(1)} %rsqrt_multiply_fusion), kind=kOutput, calls=%fused_computation.4 | convolution fusion | flops 7530872832 | bytes 24121344 | tf_op jit(solution)/shard_map/dot_general | solution.py:504
  200.8 0.0 copy-done.3
  200.8 0.6 reduce
  201.4 0.0 copy-done.1
  201.4 0.0 copy-start
  201.4 3.1 %copy-done = bf16[1024,3584]{1,0:T(8,128)(2,1)S(1)} copy-done((bf16[1024,3584]{1,0:T(8,128)(2,1)S(1)}, bf16[1024,3584]{1,0:T(8,128)(2,1)}, u32[]{:S(2)}) %copy-start) | copy-done | bytes 7340056
  204.5 0.0 copy-start.4
  204.5 10.5 %shard_map.93 = bf16[3584,1024]{1,0:T(8,128)(2,1)} custom-call(bf16[1024,3584]{1,0:T(8,128)(2,1)S(1)} %copy-done, bf16[1024,1024]{1,0:T(8,128)(2,1)S(1)} %copy-done.1), custom_call_target="tpu_custom_call" | custom-call | flops 7516192768 | bytes 14680064 | tf_op jit(solution)/shard_map/pallas_call | solution.py:510
  215.0 0.0 copy-done.4
  215.0 0.6 copy.11
  (2 shorter events, 0.0 us)
Async XLA Ops:
  0.6 4.6 %copy-start.2 = (f32[3584]{0:T(1024)S(1)}, f32[3584]{0:T(1024)}, u32[]{:S(2)}) copy-start(f32[3584]{0:T(1024)} %param.9) | copy-start | bytes 43012
  186.7 14.1 %copy-start.3 = (f32[1,3584]{1,0:T(1,128)S(1)}, f32[1,3584]{1,0:T(1,128)}, u32[]{:S(2)}) copy-start(f32[1,3584]{1,0:T(1,128)} %get-tuple-element.17) | copy-start | bytes 43012
  186.7 14.8 %copy-start.1 = (bf16[1024,1024]{1,0:T(8,128)(2,1)S(1)}, bf16[1024,1024]{1,0:T(8,128)(2,1)}, u32[]{:S(2)}) copy-start(bf16[1024,1024]{1,0:T(8,128)(2,1)} %get-tuple-element.12.gpre) | copy-start | bytes 6291460
  201.4 3.1 %copy-start = (bf16[1024,3584]{1,0:T(8,128)(2,1)S(1)}, bf16[1024,3584]{1,0:T(8,128)(2,1)}, u32[]{:S(2)}) copy-start(bf16[1024,3584]{1,0:T(8,128)(2,1)} %acts.1) | copy-start | bytes 22020100
  204.5 10.5 %copy-start.4 = (f32[1,1024]{1,0:T(1,128)S(1)}, f32[1,1024]{1,0:T(1,128)}, u32[]{:S(2)}) copy-start(f32[1,1024]{1,0:T(1,128)} %get-tuple-element.16) | copy-start | bytes 12292

commit v3 on v2

--- a/solution.py
+++ b/solution.py
@@ -288,6 +288,22 @@
         back(t, feat_copy)
         pre_chain(t, False)
 
+        p_c = t - LC
+
+        @pl.when(valid(p_c))
+        def _():
+            acte_load(p_c).start()
+            core_copy(p_c).wait_recv()
+            rows = half_of(p_c)
+
+            @pl.loop(0, width // 256)
+            def _(n):
+                cols = pl.ds(pl.multiple_of(n * 256, 256), 256)
+                own_half[rows, cols] = (
+                    own_half[rows, cols].astype(F32) + core_in[rows, cols].astype(F32)
+                ).astype(BF16)
+            x_copy(p_c).start()
+
         p_x = t - LX
 
         @pl.when(valid(p_x))
@@ -308,22 +324,6 @@
                 gerr[grows, cols] = (2.0 / tok_rows * error).astype(BF16)
             err_copy(p_x).start()
 
-        p_c = t - LC
-
-        @pl.when(valid(p_c))
-        def _():
-            acte_load(p_c).start()
-            core_copy(p_c).wait_recv()
-            rows = half_of(p_c)
-
-            @pl.loop(0, width // 256)
-            def _(n):
-                cols = pl.ds(pl.multiple_of(n * 256, 256), 256)
-                own_half[rows, cols] = (
-                    own_half[rows, cols].astype(F32) + core_in[rows, cols].astype(F32)
-                ).astype(BF16)
-            x_copy(p_c).start()
-
         @pl.when(t < NP)
         def _():
             acts_load(t).wait()
@@ -334,9 +334,9 @@
 
             rows = piece_rows(t)
 
-            @pl.loop(0, lat // 256)
-            def _(n):
-                cols = pl.ds(pl.multiple_of(n * 256, 256), 256)
+            @pl.loop(0, lat // 512)
+            def _(n):
+                cols = pl.ds(pl.multiple_of(n * 512, 512), 512)
                 part[rows, cols] = jnp.dot(
                     acts_a[t % 2], enc_v[:, cols], preferred_element_type=F32
                 )
@@ -376,9 +376,9 @@
             store(1, p_g).start()
             rows = piece_rows(p_g)
 
-            @pl.loop(0, lat // 256)
-            def _(n):
-                cols = pl.ds(pl.multiple_of(n * 256, 256), 256)
+            @pl.loop(0, lat // 512)
+            def _(n):
+                cols = pl.ds(pl.multiple_of(n * 512, 512), 512)
                 gpart[rows, cols] = lax.dot_general(
                     gerr[rows, :], dec_v[cols, :], (((1,), (1,)), ((), ())),
                     preferred_element_type=F32,

time: 216 us -> 215 us (level)
  no operation moved by 1% of the time
where the time goes in v3:
time: 215 us; the launch traced here: 214 us
  Pallas kernels  187 us (87%)
  matrix products  14.1 us (7%)
  local copies, waits for them, and re-layouts  6.11 us (3%)
  other arithmetic  5.92 us (3%)
    pallas_call x1, Pallas kernels, on_device_kernel(): pl.pallas_call(functools.partial(tokens_kernel, layer_count), out_shape=(...  177 us
    dot_general x1, matrix products, on_device_kernel(): lax.dot_general(feats, grad_error, (((0,), (0,)), ((), ())), preferred_el...  14.1 us
    pallas_call x1, Pallas kernels, on_device_kernel(): pl.pallas_call(encoder_kernel, grid=(width // tile,), out_shape=jax.Shape...  10.5 us
    reduce_sum x1, other arithmetic, on_device_kernel(): norms = jnp.sqrt(jnp.sum(dec_wide * dec_wide, axis=1) + 1e-06)  4.58 us

profile of v3, /device:TPU:0, one launch (start us, length us, event | category | flops | bytes accessed | tf_op | source)
XLA Modules:
  0.0 214.3 jit_solution(12604302435544131643)
XLA Ops:
  0.6 0.0 copy-start.2
  0.6 4.6 %fusion = f32[1024]{0:T(1024)S(1)} fusion(bf16[1024,3584]{1,0:T(8,128)(2,1)} %dec_h.1), kind=kLoop, calls=%fused_computation.2 | loop fusion | flops 11009024 | bytes 7344128 | tf_op jit(solution)/shard_map/reduce_sum | solution.py:442
  5.2 0.0 copy-done.2
  5.2 0.6 reshape.33.dbias
  5.9 0.6 broadcast_in_dim.2.norms_in
  6.5 177.0 %shard_map.92 = (bf16[1024,1024]{1,0:T(8,128)(2,1)}, bf16[1024,3584]{1,0:T(8,128)(2,1)}, bf16[1024,1024]{1,0:T(8,128)(2,1)}, f32[1,1024]{1,0:T(1,128)}, f32[1,35...) custom-call(bf16[1024,3584]{1,0:T(8,128)(2,1)} %acts.1, bf16[3584,1024]{1,0:T(8,128)(2,1)} %enc_h.1, ...), custom_call_target="tpu_custom_call" | custom-call | flops 22548578304 | bytes 29360128 | tf_op jit(solution)/shard_map/pallas_call | solution.py:448
  183.5 1.2 slice.3
  184.7 0.7 broadcast_multiply_fusion
  185.4 0.0 copy-start.3
  185.4 0.0 copy-start.1
  185.4 14.1 %fusion.2 = bf16[1024,3584]{1,0:T(8,128)(2,1)} fusion(bf16[1024,3584]{1,0:T(8,128)(2,1)} %dec_h.1, bf16[1024,1024]{1,0:T(8,128)(2,1)} %get-tuple-element.13, bf16[1024,3584]{1,0:T(8,128)(2,1)} %get-tuple-element.14, f32[1024]{0:T(1024)S(1)} %rsqrt_multiply_fusion), kind=kOutput, calls=%fused_computation.4 | convolution fusion | flops 7530872832 | bytes 24121344 | tf_op jit(solution)/shard_map/dot_general | solution.py:504
  199.5 0.0 copy-done.3
  199.5 0.6 reduce
  200.1 0.0 copy-done.1
  200.1 0.0 copy-start
  200.1 3.1 %copy-done = bf16[1024,3584]{1,0:T(8,128)(2,1)S(1)} copy-done((bf16[1024,3584]{1,0:T(8,128)(2,1)S(1)}, bf16[1024,3584]{1,0:T(8,128)(2,1)}, u32[]{:S(2)}) %copy-start) | copy-done | bytes 7340056
  203.2 0.0 copy-start.4
  203.2 10.5 %shard_map.93 = bf16[3584,1024]{1,0:T(8,128)(2,1)} custom-call(bf16[1024,3584]{1,0:T(8,128)(2,1)S(1)} %copy-done, bf16[1024,1024]{1,0:T(8,128)(2,1)S(1)} %copy-done.1), custom_call_target="tpu_custom_call" | custom-call | flops 7516192768 | bytes 14680064 | tf_op jit(solution)/shard_map/pallas_call | solution.py:510
  213.7 0.0 copy-done.4
  213.7 0.6 copy.11
  (2 shorter events, 0.0 us)
Async XLA Ops:
  0.6 4.6 %copy-start.2 = (f32[3584]{0:T(1024)S(1)}, f32[3584]{0:T(1024)}, u32[]{:S(2)}) copy-start(f32[3584]{0:T(1024)} %param.9) | copy-start | bytes 43012
  185.4 14.1 %copy-start.3 = (f32[1,3584]{1,0:T(1,128)S(1)}, f32[1,3584]{1,0:T(1,128)}, u32[]{:S(2)}) copy-start(f32[1,3584]{1,0:T(1,128)} %get-tuple-element.17) | copy-start | bytes 43012
  185.4 14.8 %copy-start.1 = (bf16[1024,1024]{1,0:T(8,128)(2,1)S(1)}, bf16[1024,1024]{1,0:T(8,128)(2,1)}, u32[]{:S(2)}) copy-start(bf16[1024,1024]{1,0:T(8,128)(2,1)} %get-tuple-element.12.gpre) | copy-start | bytes 6291460
  200.1 3.1 %copy-start = (bf16[1024,3584]{1,0:T(8,128)(2,1)S(1)}, bf16[1024,3584]{1,0:T(8,128)(2,1)}, u32[]{:S(2)}) copy-start(bf16[1024,3584]{1,0:T(8,128)(2,1)} %acts.1) | copy-start | bytes 22020100
  203.2 10.5 %copy-start.4 = (f32[1,1024]{1,0:T(1,128)S(1)}, f32[1,1024]{1,0:T(1,128)}, u32[]{:S(2)}) copy-start(f32[1,1024]{1,0:T(1,128)} %get-tuple-element.16) | copy-start | bytes 12292
